TPU v7x, 32 devices: a whole 2x2x4 slice. The times are simulated.
32 devices in a mesh: ctx: 16 (over z, y, x), head: 2 (over core).
Axes of the slice: x: 2, y: 2, z: 4, core: 2. Of those that a mesh axis runs over, the one named last changes fastest.
Arguments:
- placement: int32 [16], replicated, may hold values from 0 to 15, each once
- placed_queries: bfloat16 [4096, 4096], P('ctx', 'head'), may hold values from -160 to 160
- placed_keys: bfloat16 [4096, 1024], P('ctx', 'head'), may hold values from -4.5 to 4.5
- placed_values: bfloat16 [4096, 1024], P('ctx', 'head'), may hold values from -6 to 6
- out_weight: bfloat16 [4096, 4096], P('head', 'ctx'), may hold values from -0.125 to 0.125
Outputs:
- attention_out: bfloat16 [4096, 4096], P('ctx', 'head')
Inputs may be any that keep to these rules, and one draw needn't show every extreme that they name: placement holds each of 0 .. 15 once.
All inputs are finite; a program needn't handle non-finite values.
Results may differ from a plain program's by a relative error of at most 0.015.
Values may be sent and summed in bfloat16 or wider, within the bound.
A program may use at most 64 MiB of HBM per device.

v0:
```python
import jax
import jax.numpy as jnp
from jax import lax
from jax.sharding import PartitionSpec as P

HEAD_FEATURES = 128


masked_score = -1e30


def position_lookup(placement, device_ids):
    table = jnp.arange(placement.shape[0], dtype=jnp.int32)
    matches = device_ids[..., None] == table
    return jnp.sum(jnp.where(matches, placement, 0), axis=-1)


def attend(queries, positions, row_groups, placement, placed_keys, placed_values):
    total_rows = queries.shape[0]
    home_rows = placed_keys.shape[0]
    kv_heads = placed_keys.shape[1] // HEAD_FEATURES
    common_across = queries.shape[1] // placed_keys.shape[1]
    group_rows = total_rows // row_groups
    query_grid = queries.reshape(total_rows, kv_heads, common_across, HEAD_FEATURES)
    score_scale = HEAD_FEATURES ** (-0.5)
    initial = tuple(
        (
            (
                jnp.full((kv_heads, common_across, group_rows), masked_score, jnp.float32),
                jnp.zeros((kv_heads, common_across, group_rows), jnp.float32),
                jnp.zeros((kv_heads, common_across, group_rows, HEAD_FEATURES), jnp.float32),
            )
            for member in range(row_groups)
        )
    )

    def update(current, part_queries, part_positions, key_block, value_block, key_positions):
        running_max, running_sum, running_out = current
        scores = (
            jnp.einsum(
                "rkgd,skd->kgrs", part_queries, key_block, preferred_element_type=jnp.float32
            )
            * score_scale
        )
        allowed = key_positions[None, :] <= part_positions[:, None]
        scores = jnp.where(allowed, scores, masked_score)
        new_max = jnp.maximum(running_max, jnp.max(scores, axis=-1))
        weights = jnp.where(allowed, jnp.exp(scores - new_max[..., None]), 0.0)
        shrink = jnp.exp(running_max - new_max)
        new_sum = running_sum * shrink + jnp.sum(weights, axis=-1)
        new_out = running_out * shrink[..., None] + jnp.einsum(
            "kgrs,skd->kgrd",
            weights.astype(jnp.bfloat16),
            value_block,
            preferred_element_type=jnp.float32,
        )
        return (new_max, new_sum, new_out)

    key_piece = lax.all_gather(placed_keys, "ctx", axis=0, tiled=True)
    value_piece = lax.all_gather(placed_values, "ctx", axis=0, tiled=True)
    count = key_piece.shape[0]
    block_count = count // home_rows
    key_grid = key_piece.reshape(block_count, home_rows, kv_heads, HEAD_FEATURES)
    value_grid = value_piece.reshape(block_count, home_rows, kv_heads, HEAD_FEATURES)
    offsets = jnp.arange(block_count, dtype=jnp.int32) * home_rows

    def one_block(states, operands):
        key_block, value_block, block_first = operands
        key_index = block_first + jnp.arange(home_rows, dtype=jnp.int32)
        key_positions = (
            position_lookup(placement, key_index // home_rows) * home_rows + key_index % home_rows
        )
        earliest = jnp.min(key_positions)
        updated = [
            lax.cond(
                earliest <= jnp.max(positions),
                lambda current: update(
                    current, query_grid, positions, key_block, value_block, key_positions
                ),
                lambda current: current,
                states[0],
            )
        ]
        return (tuple(updated), None)

    finished, unused = lax.scan(one_block, initial, (key_grid, value_grid, offsets))
    outputs = [member_state[2] / member_state[1][..., None] for member_state in finished]
    joined = outputs[0]
    return (
        jnp.transpose(joined, (2, 0, 1, 3))
        .reshape(total_rows, queries.shape[1])
        .astype(jnp.bfloat16)
    )


def softmax_mixer(placement, placed_queries, placed_keys, placed_values):
    home_rows = placed_queries.shape[0]
    own_index = lax.axis_index("ctx")
    own_block = position_lookup(placement, own_index)
    positions = own_block * home_rows + jnp.arange(home_rows, dtype=jnp.int32)
    return attend(placed_queries, positions, 1, placement, placed_keys, placed_values)


def body(placement, placed_queries, placed_keys, placed_values, out_weight):
    hidden = softmax_mixer(placement, placed_queries, placed_keys, placed_values)
    partial_sum = jnp.dot(
        hidden,
        lax.all_gather(out_weight, "ctx", axis=1, tiled=True),
        preferred_element_type=jnp.float32,
    )
    rounded_term = lax.optimization_barrier(partial_sum.astype(jnp.bfloat16)).astype(jnp.float32)
    return lax.psum_scatter(
        rounded_term.astype(jnp.bfloat16), "head", scatter_dimension=1, tiled=True
    )


def solution(mesh):
    placed = (P(), P("ctx", "head"), P("ctx", "head"), P("ctx", "head"), P("head", "ctx"))
    return jax.shard_map(
        body, mesh=mesh, in_specs=placed, out_specs=P("ctx", "head"), check_vma=False
    )
```

profile of v0, /device:TPU:0, one launch (start us, length us, event | category | flops | bytes accessed | tf_op | source)
XLA Modules:
  0.0 429.1 jit_solution(15597780426701014592)
XLA Ops:
  8.8 1.3 fusion.26
  11.4 1.5 copy.17
  13.6 75.4 %all-gather.4.cloned.1.call-done = bf16[4096,512]{1,0:T(8,128)(2,1)} async-done(((bf16[256,512]{1,0:T(8,128)(2,1)}), bf16[4096,512]{1,0:T(8,128)(2,1)}) %all-gather.4.cloned.1.call-update) | async-done | bytes 4194320 | tf_op jit(solution)/shard_map/all_gather | solution.py:59
  88.9 6.9 %reshape.41 = bf16[16,256,4,128]{3,2,1,0:T(4,128)(2,1)} reshape(bf16[4096,512]{1,0:T(8,128)(2,1)} %all-gather.4.cloned.1.call-done) | data formatting | bytes 8388608 | tf_op jit(solution)/shard_map/reshape | solution.py:63
  95.9 5.3 %copy.19 = bf16[16,256,4,128]{3,1,2,0:T(8,128)(2,1)} copy(bf16[16,256,4,128]{3,2,1,0:T(4,128)(2,1)} %reshape.41) | data formatting | bytes 8388608
  101.1 65.3 %all-gather.6.cloned.1.call-done = bf16[4096,512]{1,0:T(8,128)(2,1)} async-done(((bf16[256,512]{1,0:T(8,128)(2,1)}), bf16[4096,512]{1,0:T(8,128)(2,1)}) %all-gather.6.cloned.1.call-update) | async-done | bytes 4194320 | tf_op jit(solution)/shard_map/all_gather | solution.py:60
  166.4 6.9 %reshape.42 = bf16[16,256,4,128]{3,2,1,0:T(4,128)(2,1)} reshape(bf16[4096,512]{1,0:T(8,128)(2,1)} %all-gather.6.cloned.1.call-done) | data formatting | bytes 8388608 | tf_op jit(solution)/shard_map/reshape | solution.py:64
  173.4 5.4 %copy.21 = bf16[16,256,4,128]{3,1,2,0:T(8,128)(2,1)} copy(bf16[16,256,4,128]{3,2,1,0:T(4,128)(2,1)} %reshape.42) | data formatting | bytes 8388608
  179.0 66.4 %while.17 = (s32[]{:T(128)}, f32[4,4,256]{2,1,0:T(4,128)S(1)}, f32[4,4,256]{2,1,0:T(4,128)S(1)}, f32[4,4,256,128]{3,2,1,0:T(8,128)S(1)}, s32[16]{0:T(128)S(1)}, ...) while((s32[]{:T(128)}, f32[4,4,256]{2,1,0:T(4,128)S(1)}, ...), condition=%wide.region_9.10_spmd.clone, body=%wide.region_2.9_spmd.clone.sunk | while | flops 551644928 | bytes 18885992 | solution.py:86
  180.3 1.3 fusion.33
  182.8 5.8 %conditional.3 = ((f32[4,4,256]{2,1,0:T(4,128)S(1)}, f32[4,4,256]{2,1,0:T(4,128)S(1)}, f32[4,4,256,128]{3,2,1,0:T(8,128)S(1)})) conditional(s32[]{:T(128)} %convert_element_type.37, (f32[4,4,256]{2,1,0:T(4,128)S(1)}, f32[4,4,256]{2,1,0:T(4,128)S(1)}, f32[4,4,256,128]{3,2,1,0:T(8,128)S(1)}) %tuple.54, (s32[256]{0:T(256)S(1)}, s32[]{:T(128)}, ...), branch_computations={%region_5.5_spmd, %region_6.8_spmd} | conditional | flops 551624960 | bytes 18879524 | solution.py:75
  182.9 1.7 fusion.2
  185.7 2.9 multiply_add_fusion
  189.9 1.3 fusion.33
  193.7 1.3 fusion.33
  197.5 1.3 fusion.33
  201.3 1.3 fusion.33
  205.1 1.3 fusion.33
  235.4 1.3 fusion.33
  245.5 1.9 copy.22
  247.3 1.8 divide_convert_fusion
  249.1 153.9 %all-gather.8.cloned.1.call-done = bf16[2048,4096]{1,0:T(8,128)(2,1)} async-done(((bf16[2048,256]{1,0:T(8,128)(2,1)}), bf16[2048,4096]{1,0:T(8,128)(2,1)}) %all-gather.8.cloned.1.call-update) | async-done | bytes 16777232 | tf_op jit(solution)/shard_map/all_gather | solution.py:108
  403.1 11.6 %convolution_convert_fusion = bf16[256,4096]{1,0:T(8,128)(2,1)} fusion(bf16[256,2048]{0,1:T(8,128)(2,1)S(1)} %bitcast.44, bf16[2048,4096]{1,0:T(8,128)(2,1)} %all-gather.8.cloned.1.call-done), kind=kOutput, calls=%fused_computation.38 | convolution fusion | flops 4296015872 | bytes 19922944 | tf_op jit(solution)/shard_map/dot_general | solution.py:106
  414.7 8.0 %reduce-scatter.2.cloned.1.call-done = bf16[256,2048]{1,0:T(8,128)(2,1)} async-done(((bf16[256,4096]{1,0:T(8,128)(2,1)}), bf16[256,2048]{1,0:T(8,128)(2,1)}) %reduce-scatter.2.cloned.1.call-update) | async-done | bytes 1048592 | tf_op jit(solution)/shard_map/reduce_scatter | solution.py:112
  (110 shorter events, 37.5 us)
Async XLA Ops:
  6.5 82.4 %all-gather.4.cloned.1.call-start = ((), (), s32[]{:S(2)}) async-start(), calls=%async_computation.1 | async-start | bytes 4456448 | tf_op jit(solution)/shard_map/all_gather | solution.py:59
  7.3 159.2 %all-gather.6.cloned.1.call-start = ((), (), s32[]{:S(2)}) async-start(), calls=%async_computation.2 | async-start | bytes 4456448 | tf_op jit(solution)/shard_map/all_gather | solution.py:60
  8.0 395.1 %all-gather.8.cloned.1.call-start = ((), (), s32[]{:S(2)}) async-start(), calls=%async_computation.3 | async-start | bytes 17825792 | tf_op jit(solution)/shard_map/all_gather | solution.py:108
  8.7 413.9 %reduce-scatter.2.cloned.1.call-start = ((), (), s32[]{:S(2)}) async-start(), calls=%async_computation.4 | async-start | bytes 3145728 | tf_op jit(solution)/shard_map/reduce_scatter | solution.py:112
  173.4 5.6 %copy-start = (s32[16]{0:T(128)S(1)}, s32[16]{0:T(128)}, u32[]{:S(2)}) copy-start(s32[16]{0:T(128)} %param.9) | copy-start | bytes 196
Sparse Core Ops, SparseCore 0:
  10.1 78.7 all-gather.3
  91.7 74.6 all-gather.5
  169.2 233.8 all-gather.7
  414.8 7.7 reduce-scatter.1
where the time goes:
time: 431 us; the launch traced here: 429 us
  waiting for transfers between devices  305 us (71%)
  local copies, waits for them, and re-layouts  38.4 us (9%)
  other arithmetic  36.5 us (8%)
  loops' own time  19.5 us (5%)
  matrix products  16.1 us (4%)
  between operations  13.9 us (3%)
    all_gather x1, waiting for transfers between devices, body(): lax.all_gather(out_weight, 'ctx', axis=1, tiled=True)  154 us
    all_gather x1, waiting for transfers between devices, attend(): key_piece = lax.all_gather(placed_keys, 'ctx', axis=0, tiled=True)  75.4 us
    all_gather x1, waiting for transfers between devices, attend(): value_piece = lax.all_gather(placed_values, 'ctx', axis=0, tiled=True)  65.3 us
    reduce_min x16, other arithmetic, one_block(): earliest = jnp.min(key_positions)  20.1 us
    another operation x1, loops' own time, attend(): lax.scan(one_block, initial, (key_grid, value_grid, offsets))  19.3 us
    unnamed x6, local copies, waits for them, and re-layouts  12.8 us
    dot_general x1, matrix products, body(): jnp.dot(hidden, lax.all_gather(out_weight, 'ctx', axis=1, tiled=True), pr...  11.6 us
    select_n x16, other arithmetic, one_block(): key_index // home_rows  10.1 us
  transfers between devices with their start and end apart: 4, of which 4 were waited for; matrix products, arithmetic and copies ran while one was open for 19% of the time, Pallas kernels for 0%

commit v1 on v0

v1 whole, which is shorter than its diff:
```python
import functools

import jax
import jax.numpy as jnp
from jax import lax
from jax.experimental import pallas as pl
from jax.experimental.pallas import tpu as pltpu
from jax.sharding import PartitionSpec as P

HEAD_FEATURES = 128
PLANE = 4
LOG2_E = 1.4426950408889634
MESH = pl.DeviceIdType.MESH
lowest = -1e30
vmem_limit = 60 * 1024 * 1024


def attend_kernel(scale, place_ref, own_ref, q_ref, k_ref, v_ref, o_ref, stacked, peak, total, acc):
    blocks, rows, _ = k_ref.shape
    heads = q_ref.shape[1] // HEAD_FEATURES
    for i in range(heads):
        stacked[i * rows:(i + 1) * rows, :] = q_ref[:, i * HEAD_FEATURES:(i + 1) * HEAD_FEATURES]
    peak[...] = jnp.full_like(peak, lowest)
    total[...] = jnp.zeros_like(total)
    acc[...] = jnp.zeros_like(acc)
    mine = own_ref[0]

    def update(j, diagonal):
        keys = k_ref[j]
        values = v_ref[j]
        for i in range(heads):
            cols = slice(i * rows, (i + 1) * rows)
            scores = lax.dot_general(
                keys, stacked[cols, :], (((1,), (1,)), ((), ())), preferred_element_type=jnp.float32
            )
            if diagonal:
                key_at = lax.broadcasted_iota(jnp.int32, scores.shape, 0)
                query_at = lax.broadcasted_iota(jnp.int32, scores.shape, 1)
                scores = jnp.where(key_at <= query_at, scores, lowest)
            old = peak[:, cols]
            new = jnp.maximum(old, jnp.max(scores, axis=0, keepdims=True))
            weights = jnp.exp2((scores - new) * scale)
            shrink = jnp.exp2((old - new) * scale)
            peak[:, cols] = new
            total[:, cols] = total[:, cols] * shrink + jnp.sum(weights, axis=0, keepdims=True)
            acc[:, cols] = acc[:, cols] * shrink + lax.dot_general(
                values, weights.astype(jnp.bfloat16), (((0,), (0,)), ((), ())),
                preferred_element_type=jnp.float32,
            )

    def step(j, carry):
        at = place_ref[j]

        @pl.when(at < mine)
        def _():
            update(j, False)

        @pl.when(at == mine)
        def _():
            update(j, True)

        return carry

    lax.fori_loop(0, blocks, step, 0)
    for i in range(heads):
        cols = slice(i * rows, (i + 1) * rows)
        out = acc[:, cols] / total[:, cols]
        o_ref[:, i * HEAD_FEATURES:(i + 1) * HEAD_FEATURES] = out.T.astype(o_ref.dtype)


def attend(placement, own_block, queries, keys, values):
    blocks, rows, width = keys.shape
    kv_heads = width // HEAD_FEATURES
    group = queries.shape[1] // kv_heads
    common = group // HEAD_FEATURES
    scale = HEAD_FEATURES ** (-0.5) * LOG2_E
    return pl.pallas_call(
        functools.partial(attend_kernel, scale),
        out_shape=jax.ShapeDtypeStruct(queries.shape, queries.dtype),
        grid_spec=pltpu.PrefetchScalarGridSpec(
            num_scalar_prefetch=2,
            grid=(kv_heads,),
            in_specs=[
                pl.BlockSpec((rows, group), lambda g, *_: (0, g)),
                pl.BlockSpec((blocks, rows, HEAD_FEATURES), lambda g, *_: (0, 0, g)),
                pl.BlockSpec((blocks, rows, HEAD_FEATURES), lambda g, *_: (0, 0, g)),
            ],
            out_specs=pl.BlockSpec((rows, group), lambda g, *_: (0, g)),
            scratch_shapes=[
                pltpu.VMEM((common * rows, HEAD_FEATURES), jnp.bfloat16),
                pltpu.VMEM((1, common * rows), jnp.float32),
                pltpu.VMEM((1, common * rows), jnp.float32),
                pltpu.VMEM((HEAD_FEATURES, common * rows), jnp.float32),
            ],
        ),
        compiler_params=pltpu.CompilerParams(vmem_limit_bytes=vmem_limit),
        cost_estimate=pl.CostEstimate(
            flops=4 * blocks * rows * rows * queries.shape[1],
            bytes_accessed=4 * (keys.size + queries.size),
            transcendentals=blocks * rows * rows * kv_heads * common,
        ),
    )(placement, own_block, queries, keys, values)


def place_of(depth):
    me = lax.axis_index("ctx")
    z = me // PLANE
    p = me % PLANE
    flip_x = p + 1 - 2 * (p % 2)
    flip_y = (p + 2) % PLANE
    return z, p, flip_x, flip_y, (flip_x + 2) % PLANE


class Copies:
    def __init__(self):
        self.started = []

    def start(self, condition, make):
        @pl.when(condition)
        def _():
            make().start()

        self.started.append((condition, make))

    def finish(self):
        for condition, make in self.started:
            @pl.when(condition)
            def _(make=make):
                make().wait_send()


def remote(src, dst, send, recv, target):
    return pltpu.make_async_remote_copy(
        src_ref=src, dst_ref=dst, send_sem=send, recv_sem=recv,
        device_id={"ctx": target}, device_id_type=MESH,
    )


def gather_kernel(depth, half, k_ref, v_ref, w_ref, k_all, v_all, w_all,
                  own_sem, line_send, plane_send, relay_send, recv, w_send, w_recv):
    z, p, px, py, pd = place_of(depth)
    me = z * PLANE + p
    barrier = pltpu.get_barrier_semaphore()
    greeted = (
        z * PLANE + px, z * PLANE + py,
        (z + 1) % depth * PLANE + p, (z + depth - 1) % depth * PLANE + p,
    )
    for other in greeted:
        pl.semaphore_signal(barrier, inc=1, device_id={"ctx": other}, device_id_type=MESH)
    pl.semaphore_wait(barrier, len(greeted))

    w_own = w_ref.at[pl.ds(0, half), :]
    locals_ = [
        pltpu.make_async_copy(k_ref, k_all.at[me], own_sem.at[0]),
        pltpu.make_async_copy(v_ref, v_all.at[me], own_sem.at[1]),
        pltpu.make_async_copy(w_own, w_all.at[z], own_sem.at[2]),
    ]
    copies = Copies()
    pairs = ((k_ref, k_all), (v_ref, v_all))

    def arrived(array, source):
        ref = pairs[array][1].at[source]
        remote(ref, ref, own_sem.at[0], recv.at[array, source], me).wait_recv()

    def move(array, source, own, send, target):
        dst = pairs[array][1].at[source]
        src = pairs[array][0] if own else dst
        return remote(src, dst, send, recv.at[array, source], target)

    def line(array, zs, own, up):
        target = (z + 1 if up else z - 1) * PLANE + p
        return move(array, zs * PLANE + p, own, line_send.at[array, zs, int(up)], target)

    def plane(array, zs, own, axis):
        target = z * PLANE + (px if axis == 0 else py)
        return move(array, zs * PLANE + p, own, plane_send.at[array, zs, axis], target)

    def relay(array, zs):
        source, target = (px, py) if array == 0 else (py, px)
        return move(array, zs * PLANE + source, False, relay_send.at[array, zs], z * PLANE + target)

    def weight(zs, own, up):
        target = (z + 1 if up else z - 1) * PLANE + p
        dst = w_all.at[zs]
        return remote(w_own if own else dst, dst, w_send.at[zs, int(up)], w_recv.at[zs], target)

    above = z + 1 < depth
    below = z > 0
    always = z >= 0
    for array in range(2):
        copies.start(above, functools.partial(line, array, z, True, True))
        copies.start(below, functools.partial(line, array, z, True, False))
    for array in range(2):
        for axis in range(2):
            copies.start(always, functools.partial(plane, array, z, True, axis))
    for copy in locals_:
        copy.start()

    def pass_on(t):
        for up in (True, False):
            zs = z - t if up else z + t
            there = z >= t if up else zs < depth

            @pl.when(there)
            def _(zs=zs):
                for array in range(2):
                    arrived(array, zs * PLANE + p)

            on = there & (above if up else below)
            for array in range(2):
                copies.start(on, functools.partial(line, array, zs, False, up))
            for array in range(2):
                for axis in range(2):
                    copies.start(there, functools.partial(plane, array, zs, False, axis))

    def pass_across(t):
        for up in (True, False)[: 1 if t == 0 else 2]:
            zs = z - t if up else z + t
            there = z >= t if up else zs < depth

            @pl.when(there)
            def _(zs=zs):
                arrived(0, zs * PLANE + px)
                arrived(1, zs * PLANE + py)

            for array in range(2):
                copies.start(there, functools.partial(relay, array, zs))

    def pass_weight(t):
        if t == 0:
            copies.start(above, functools.partial(weight, z, True, True))
            copies.start(below, functools.partial(weight, z, True, False))
            return
        for up in (True, False):
            zs = z - t if up else z + t
            there = z >= t if up else zs < depth

            @pl.when(there)
            def _(zs=zs):
                remote(w_all.at[zs], w_all.at[zs], own_sem.at[0], w_recv.at[zs], me).wait_recv()

            copies.start(there & (above if up else below), functools.partial(weight, zs, False, up))

    for t in range(1, depth):
        pass_on(t)
        pass_weight(t - 1)
        pass_across(t - 1)
    pass_across(depth - 1)
    pass_weight(depth - 1)
    for zs in range(depth):
        arrived(1, zs * PLANE + px)
        arrived(0, zs * PLANE + py)
        arrived(0, zs * PLANE + pd)
        arrived(1, zs * PLANE + pd)
    for copy in locals_:
        copy.wait()
    copies.finish()


def gather(depth, half, keys, values, weight):
    blocks = depth * PLANE
    dma = pltpu.SemaphoreType.DMA
    anywhere = pl.BlockSpec(memory_space=pl.ANY)
    return pl.pallas_call(
        functools.partial(gather_kernel, depth, half),
        out_shape=(
            jax.ShapeDtypeStruct((blocks,) + keys.shape, keys.dtype),
            jax.ShapeDtypeStruct((blocks,) + values.shape, values.dtype),
            jax.ShapeDtypeStruct((depth, half, weight.shape[1]), weight.dtype),
        ),
        in_specs=[anywhere] * 3,
        out_specs=(anywhere,) * 3,
        scratch_shapes=[
            dma((3,)), dma((2, depth, 2)), dma((2, depth, 2)), dma((2, depth)),
            dma((2, blocks)), dma((depth, 2)), dma((depth,)),
        ],
        compiler_params=pltpu.CompilerParams(
            collective_id=0, has_side_effects=True, vmem_limit_bytes=vmem_limit
        ),
    )(keys, values, weight)


def project_kernel(depth, half, hid_ref, w_ref, w_first, out_ref,
                   hid, w_late, theirs, mine_half, other_half, final, landed,
                   own_sem, hid_send, relay_send, hid_recv, w_send, w_recv,
                   core_send, core_recv, out_send, out_recv):
    z, p, px, py, pd = place_of(depth)
    me = z * PLANE + p
    core = lax.axis_index("head")
    rows = hid_ref.shape[0]
    cols = w_ref.shape[1]
    share = depth // 2
    barrier = pltpu.get_barrier_semaphore()
    greeted = (
        z * PLANE + px, z * PLANE + py, z * PLANE + pd,
        (z + 1) % depth * PLANE + p, (z + depth - 1) % depth * PLANE + p,
    )
    for other in greeted:
        pl.semaphore_signal(barrier, inc=1, device_id={"ctx": other}, device_id_type=MESH)
    pl.semaphore_signal(barrier, inc=1, device_id={"head": 1 - core}, device_id_type=MESH)
    pl.semaphore_wait(barrier, len(greeted) + 1)

    copies = Copies()
    always = z >= 0
    above = z + 1 < depth
    below = z > 0
    own_parts = [hid_ref.at[:, pl.ds(s * half, half)] for s in range(2)]
    w_own = w_ref.at[pl.ds(half, half), :]

    def send_hidden(part, axis):
        target = z * PLANE + (px if axis == 0 else py)
        return remote(own_parts[part], hid.at[p, part], hid_send.at[part, axis], hid_recv.at[p, part], target)

    def relay_hidden(part):
        source, target = (px, py) if part == 0 else (py, px)
        slot = hid.at[source, part]
        return remote(slot, slot, relay_send.at[part], hid_recv.at[source, part], z * PLANE + target)

    def hidden_arrived(source, part):
        slot = hid.at[source, part]
        remote(slot, slot, own_sem.at[0], hid_recv.at[source, part], me).wait_recv()

    def weight(zs, own, up):
        target = (z + 1 if up else z - 1) * PLANE + p
        dst = w_late.at[zs]
        return remote(w_own if own else dst, dst, w_send.at[zs, int(up)], w_recv.at[zs], target)

    for part in range(2):
        copies.start(always, functools.partial(send_hidden, part, part))
    copies.start(above, functools.partial(weight, z, True, True))
    copies.start(below, functools.partial(weight, z, True, False))
    for part in range(2):
        copies.start(always, functools.partial(send_hidden, part, 1 - part))
    locals_ = [pltpu.make_async_copy(own_parts[s], hid.at[p, s], own_sem.at[s]) for s in range(2)]
    locals_.append(pltpu.make_async_copy(w_own, w_late.at[z], own_sem.at[2]))
    for copy in locals_:
        copy.start()

    def pass_weight(t):
        for up in (True, False):
            zs = z - t if up else z + t
            there = z >= t if up else zs < depth

            @pl.when(there)
            def _(zs=zs):
                remote(w_late.at[zs], w_late.at[zs], own_sem.at[0], w_recv.at[zs], me).wait_recv()

            copies.start(there & (above if up else below), functools.partial(weight, zs, False, up))

    for t in range(1, depth):
        pass_weight(t)
        if t == 1:
            for part in range(2):
                hidden_arrived(px if part == 0 else py, part)
                copies.start(always, functools.partial(relay_hidden, part))
    for copy in locals_:
        copy.wait()

    def term(source, chunk):
        return (
            jnp.dot(hid[source, 0], w_first[chunk], preferred_element_type=jnp.float32)
            + jnp.dot(hid[source, 1], w_late[chunk], preferred_element_type=jnp.float32)
        ).astype(jnp.bfloat16)

    def core_copy(slot):
        return pltpu.make_async_remote_copy(
            src_ref=other_half.at[slot], dst_ref=theirs.at[slot],
            send_sem=core_send.at[slot], recv_sem=core_recv.at[slot],
            device_id={"head": 1 - core}, device_id_type=MESH,
        )

    def finished(slot, target):
        return remote(final.at[slot], landed.at[p], out_send.at[slot], out_recv.at[p], z * PLANE + target)

    order = (p, px, py, pd)

    def settle(slot):
        core_copy(slot).wait_recv()
        summed = (
            mine_half[slot].astype(jnp.float32) + theirs[slot].astype(jnp.float32)
        ).astype(jnp.bfloat16)
        if slot == 0:
            landed[p] = summed
        else:
            final[slot] = summed
            copies.start(always, functools.partial(finished, slot, order[slot]))

    for slot, source in enumerate(order):
        if slot in (1, 2):
            hidden_arrived(source, 2 - slot)
        if slot == 3:
            hidden_arrived(source, 0)
            hidden_arrived(source, 1)
        for j in range(share):
            other_half[slot, j] = term(source, (1 - core) * share + j)
        core_copy(slot).start()
        for j in range(share):
            mine_half[slot, j] = term(source, core * share + j)
        if slot:
            settle(slot - 1)
    settle(PLANE - 1)
    for slot in range(1, PLANE):
        source = order[slot]
        remote(landed.at[source], landed.at[source], own_sem.at[0], out_recv.at[source], me).wait_recv()
    for source in range(PLANE):
        for j in range(share):
            at = (j * PLANE + source) * cols
            out_ref[:, at:at + cols] = landed[source, j]
    for slot in range(PLANE):
        core_copy(slot).wait_send()
    copies.finish()


def project(depth, half, hidden, weight, w_first):
    rows, width = hidden.shape
    cols = weight.shape[1]
    share = depth // 2
    dma = pltpu.SemaphoreType.DMA
    vmem = pl.BlockSpec(memory_space=pltpu.VMEM)
    block = pltpu.VMEM((PLANE, share, rows, cols), jnp.bfloat16)
    return pl.pallas_call(
        functools.partial(project_kernel, depth, half),
        out_shape=jax.ShapeDtypeStruct((rows, share * PLANE * cols), hidden.dtype),
        in_specs=[vmem] * 3,
        out_specs=vmem,
        scratch_shapes=[
            pltpu.VMEM((PLANE, 2, rows, half), jnp.bfloat16),
            pltpu.VMEM((depth, half, cols), jnp.bfloat16),
            block, block, block, block, block,
            dma((3,)), dma((2, 2)), dma((2,)), dma((PLANE, 2)), dma((depth, 2)), dma((depth,)),
            dma((PLANE,)), dma((PLANE,)), dma((PLANE,)), dma((PLANE,)),
        ],
        compiler_params=pltpu.CompilerParams(
            collective_id=1, has_side_effects=True, vmem_limit_bytes=vmem_limit
        ),
    )(hidden, weight, w_first)


def body(fast, placement, queries, keys, values, weight):
    blocks = placement.shape[0]
    depth = blocks // PLANE
    half = weight.shape[0] // 2
    table = jnp.arange(blocks, dtype=jnp.int32)
    own_block = jnp.sum(jnp.where(table == lax.axis_index("ctx"), placement, 0))[None]
    if fast:
        all_keys, all_values, w_first = gather(depth, half, keys, values, weight)
    else:
        all_keys = lax.all_gather(keys, "ctx", axis=0)
        all_values = lax.all_gather(values, "ctx", axis=0)
    hidden = attend(placement, own_block, queries, all_keys, all_values)
    if fast:
        return project(depth, half, hidden, weight, w_first)
    partial_sum = jnp.dot(
        hidden,
        lax.all_gather(weight, "ctx", axis=1, tiled=True),
        preferred_element_type=jnp.float32,
    )
    term = lax.optimization_barrier(partial_sum.astype(jnp.bfloat16))
    return lax.psum_scatter(term, "head", scatter_dimension=1, tiled=True)


def solution(mesh):
    placed = (P(), P("ctx", "head"), P("ctx", "head"), P("ctx", "head"), P("head", "ctx"))
    fast = mesh.shape["head"] == 2 and mesh.shape["ctx"] == 4 * PLANE
    return jax.shard_map(
        functools.partial(body, fast), mesh=mesh, in_specs=placed,
        out_specs=P("ctx", "head"), check_vma=False,
    )
```

time: 431 us -> 226 us (0.52)
  waiting for transfers between devices: 305 us -> 0 us
  Pallas kernels: 0 us -> 223 us
  local copies, waits for them, and re-layouts: 38.4 us -> 2.3 us
  other arithmetic: 36.5 us -> 1.35 us
  loops' own time: 19.5 us -> 0 us
  matrix products: 16.1 us -> 0 us
  between operations: 13.9 us -> 0.02 us
    all_gather x3 -> x0, waiting for transfers between devices: 295 us -> none  [the longest x1 154 us: body(): lax.all_gather(out_weight, 'ctx', axis=1, tiled=True)]
    pallas_call x0 -> x3, Pallas kernels: none -> 223 us  [the longest x1 135 us: project(): pl.pallas_call(functools.partial(project_kernel, depth, half), out_shape=...]
    reduce_min x16 -> x0, other arithmetic: 20.1 us -> none  [one_block(): earliest = jnp.min(key_positions)]
    another operation x17 -> x0, loops' own time: 19.5 us -> none  [the longest x1 19.3 us: attend(): lax.scan(one_block, initial, (key_grid, value_grid, offsets))]
    dot_general x3 -> x0, matrix products: 16.1 us -> none  [the longest x1 11.6 us: body(): jnp.dot(hidden, lax.all_gather(out_weight, 'ctx', axis=1, tiled=True), pr...]
    reshape x2 -> x0, local copies, waits for them, and re-layouts: 13.9 us -> none  [the longest x1 6.94 us: attend(): value_piece.reshape(block_count, home_rows, kv_heads, HEAD_FEATURES)]
    unnamed x6 -> x1, local copies, waits for them, and re-layouts: 12.8 us -> 2.3 us
    select_n x16 -> x0, other arithmetic: 10.1 us -> none  [one_block(): key_index // home_rows]
  transfers between devices with their start and end apart: 4 -> 0, of which waited for: 4 -> 0; matrix products, arithmetic and copies ran while one was open for 19% -> 0% of each run, Pallas kernels for 0% -> 0%
where the time goes in v1:
time: 226 us; the launch traced here: 227 us
  Pallas kernels  223 us (99%)
  local copies, waits for them, and re-layouts  2.3 us (1%)
    pallas_call x1, Pallas kernels, project(): pl.pallas_call(functools.partial(project_kernel, depth, half), out_shape=...  135 us
    pallas_call x1, Pallas kernels, gather(): pl.pallas_call(functools.partial(gather_kernel, depth, half), out_shape=(...  77 us
    pallas_call x1, Pallas kernels, attend(): pl.pallas_call(functools.partial(attend_kernel, scale), out_shape=jax.Sha...  11 us

profile of v1, /device:TPU:0, one launch (start us, length us, event | category | flops | bytes accessed | tf_op | source)
XLA Modules:
  0.0 226.9 jit_solution(598440405370133277)
XLA Ops:
  0.0 1.4 fusion
  1.4 77.0 %shard_map.55 = (bf16[16,256,512]{2,1,0:T(8,128)(2,1)}, bf16[16,256,512]{2,1,0:T(8,128)(2,1)}, bf16[4,1024,256]{2,1,0:T(8,128)(2,1)}) custom-call(bf16[256,512]{1,0:T(8,128)(2,1)} %k_ref.1, bf16[256,512]{1,0:T(8,128)(2,1)} %v_ref.1, bf16[2048,256]{1,0:T(8,128)(2,1)} %w_ref.3), custom_call_target="tpu_custom_call" | custom-call | tf_op jit(solution)/shard_map/pallas_call | solution.py:264
  78.4 11.0 %shard_map.56.hid_ref = bf16[256,2048]{1,0:T(8,128)(2,1)} custom-call(s32[16]{0:T(128)} %place_ref.1, s32[1]{0:T(128)} %bitcast.own_ref, bf16[256,2048]{1,0:T(8,128)(2,1)} %q_ref.1, bf16[16,256,512]{2,1,0:T(8,128)(2,1)} %get-tuple-element.8.k_ref, bf16[16,256,512]{2,1,0:T(8,128)(2,1)} %get-tuple-element.9.v_ref), custom_call_target="tpu_custom_call" | custom-call | flops 8589934592 | bytes 10485760 | tf_op jit(solution)/shard_map/pallas_call | solution.py:77
  89.4 135.2 %shard_map.57 = bf16[256,2048]{1,0:T(8,128)(2,1)} custom-call(bf16[256,2048]{1,0:T(8,128)(2,1)} %shard_map.56.hid_ref, bf16[2048,256]{1,0:T(8,128)(2,1)} %w_ref.3, bf16[4,1024,256]{2,1,0:T(8,128)(2,1)} %get-tuple-element.10.w_first), custom_call_target="tpu_custom_call" | custom-call | tf_op jit(solution)/shard_map/pallas_call | solution.py:421
  224.6 2.3 %copy.7 = bf16[256,2048]{1,0:T(8,128)(2,1)} copy(bf16[256,2048]{1,0:T(8,128)(2,1)} %shard_map.57) | data formatting | bytes 2097152

commit v2 on v1

--- a/solution.py
+++ b/solution.py
@@ -136,8 +136,9 @@
     )
 
 
-def gather_kernel(depth, half, k_ref, v_ref, w_ref, k_all, v_all, w_all,
-                  own_sem, line_send, plane_send, relay_send, recv, w_send, w_recv):
+def gather_attend_kernel(depth, half, scale, place_ref, q_ref, k_ref, v_ref, w_ref, o_ref, w_all,
+                         k_all, v_all, turned, peak, total, acc,
+                         own_sem, line_send, plane_send, relay_send, recv, w_send, w_recv):
     z, p, px, py, pd = place_of(depth)
     me = z * PLANE + p
     barrier = pltpu.get_barrier_semaphore()
@@ -150,11 +151,7 @@
     pl.semaphore_wait(barrier, len(greeted))
 
     w_own = w_ref.at[pl.ds(0, half), :]
-    locals_ = [
-        pltpu.make_async_copy(k_ref, k_all.at[me], own_sem.at[0]),
-        pltpu.make_async_copy(v_ref, v_all.at[me], own_sem.at[1]),
-        pltpu.make_async_copy(w_own, w_all.at[z], own_sem.at[2]),
-    ]
+    w_local = pltpu.make_async_copy(w_own, w_all.at[z], own_sem.at[0])
     copies = Copies()
     pairs = ((k_ref, k_all), (v_ref, v_all))
 
@@ -187,26 +184,27 @@
     above = z + 1 < depth
     below = z > 0
     always = z >= 0
+    reach = {}
+    for t in range(depth):
+        reach[t, True] = z - t, z >= t, (z >= t) & above
+        reach[t, False] = z + t, z + t < depth, (z + t < depth) & below
     for array in range(2):
         copies.start(above, functools.partial(line, array, z, True, True))
         copies.start(below, functools.partial(line, array, z, True, False))
     for array in range(2):
         for axis in range(2):
             copies.start(always, functools.partial(plane, array, z, True, axis))
-    for copy in locals_:
-        copy.start()
+    w_local.start()
 
     def pass_on(t):
         for up in (True, False):
-            zs = z - t if up else z + t
-            there = z >= t if up else zs < depth
+            zs, there, on = reach[t, up]
 
             @pl.when(there)
             def _(zs=zs):
                 for array in range(2):
                     arrived(array, zs * PLANE + p)
 
-            on = there & (above if up else below)
             for array in range(2):
                 copies.start(on, functools.partial(line, array, zs, False, up))
             for array in range(2):
@@ -215,8 +213,7 @@
 
     def pass_across(t):
         for up in (True, False)[: 1 if t == 0 else 2]:
-            zs = z - t if up else z + t
-            there = z >= t if up else zs < depth
+            zs, there, on = reach[t, up]
 
             @pl.when(there)
             def _(zs=zs):
@@ -232,52 +229,142 @@
             copies.start(below, functools.partial(weight, z, True, False))
             return
         for up in (True, False):
-            zs = z - t if up else z + t
-            there = z >= t if up else zs < depth
+            zs, there, on = reach[t, up]
 
             @pl.when(there)
             def _(zs=zs):
                 remote(w_all.at[zs], w_all.at[zs], own_sem.at[0], w_recv.at[zs], me).wait_recv()
 
-            copies.start(there & (above if up else below), functools.partial(weight, zs, False, up))
-
-    for t in range(1, depth):
-        pass_on(t)
-        pass_weight(t - 1)
-        pass_across(t - 1)
-    pass_across(depth - 1)
-    pass_weight(depth - 1)
-    for zs in range(depth):
-        arrived(1, zs * PLANE + px)
-        arrived(0, zs * PLANE + py)
-        arrived(0, zs * PLANE + pd)
-        arrived(1, zs * PLANE + pd)
-    for copy in locals_:
-        copy.wait()
+            copies.start(on, functools.partial(weight, zs, False, up))
+
+    rows = q_ref.shape[0]
+    heads = q_ref.shape[1] // HEAD_FEATURES
+    common = q_ref.shape[1] // k_ref.shape[1]
+
+    def features(h):
+        return slice(h * HEAD_FEATURES, (h + 1) * HEAD_FEATURES)
+
+    for h in range(heads):
+        turned[h] = q_ref[:, features(h)].T
+
+    def update(read_keys, read_values, bias, first):
+        def score(h):
+            return jnp.dot(
+                read_keys(features(h // common)), turned[h], preferred_element_type=jnp.float32
+            )
+
+        following = score(0)
+        for h in range(heads):
+            scores = following
+            if h + 1 < heads:
+                following = score(h + 1)
+            if h % common == 0:
+                values = read_values(features(h // common)).T
+            if first:
+                key_at = lax.broadcasted_iota(jnp.int32, scores.shape, 0)
+                query_at = lax.broadcasted_iota(jnp.int32, scores.shape, 1)
+                scores = jnp.where(key_at <= query_at, scores, lowest)
+                new = jnp.max(scores, axis=0, keepdims=True)
+                weights = jnp.exp2((scores - new) * scale)
+            else:
+                old = peak[h]
+                new = jnp.maximum(old, jnp.max(scores, axis=0, keepdims=True) + bias)
+                weights = jnp.exp2((scores - (new - bias)) * scale)
+                shrink = jnp.exp2((old - new) * scale)
+            sums = jnp.sum(weights, axis=0, keepdims=True)
+            part = jnp.dot(values, weights.astype(jnp.bfloat16), preferred_element_type=jnp.float32)
+            peak[h] = new
+            if first:
+                total[h] = sums
+                acc[h] = part
+            else:
+                total[h] = total[h] * shrink + sums
+                acc[h] = acc[h] * shrink + part
+
+    update(lambda f: k_ref[:, f], lambda f: v_ref[:, f], 0.0, True)
+    pass_on(1)
+    pass_weight(0)
+    pass_across(0)
+
+    near = z - 1 + 2 * ((depth - 1 - z) // (depth - 1))
+    last = (depth - 1) * (1 - z // 2)
+    third = depth * (depth - 1) // 2 - z - near - last
+    services = {
+        3: ((pass_on, 2),),
+        4: ((pass_across, 1), (pass_weight, 1)),
+        6: ((pass_on, 3),),
+        8: ((pass_across, 2), (pass_weight, 2)),
+        12: ((pass_across, 3), (pass_weight, 3)),
+    }
+
+    def step(n, carry):
+        for at, calls in services.items():
+            @pl.when(n == at)
+            def _(calls=calls):
+                for call, t in calls:
+                    call(t)
+
+        r = n // PLANE
+        s = n % PLANE
+        zs = jnp.where(r == 0, z, jnp.where(r == 1, near, jnp.where(r == 2, third, last)))
+        source = zs * PLANE + (p // 2 + s // 2) % 2 * 2 + (p % 2 + s % 2) % 2
+
+        @pl.when(s == 1)
+        def _():
+            arrived(1, source)
+
+        @pl.when(s == 2)
+        def _():
+            arrived(0, source)
+
+        @pl.when(s == 3)
+        def _():
+            arrived(0, source)
+            arrived(1, source)
+
+        bias = jnp.where(place_ref[source] < place_ref[me], 0.0, lowest)
+        update(
+            lambda f: k_all[source, :, f], lambda f: v_all[source, :, f], bias, False
+        )
+        return carry
+
+    lax.fori_loop(1, depth * PLANE, step, 0)
+    for h in range(heads):
+        o_ref[:, features(h)] = (acc[h] / total[h]).T.astype(o_ref.dtype)
+    w_local.wait()
     copies.finish()
 
 
-def gather(depth, half, keys, values, weight):
+def gather_attend(depth, half, placement, queries, keys, values, weight):
     blocks = depth * PLANE
+    rows = queries.shape[0]
+    heads = queries.shape[1] // HEAD_FEATURES
+    scale = HEAD_FEATURES ** (-0.5) * LOG2_E
     dma = pltpu.SemaphoreType.DMA
     anywhere = pl.BlockSpec(memory_space=pl.ANY)
+    vmem = pl.BlockSpec(memory_space=pltpu.VMEM)
     return pl.pallas_call(
-        functools.partial(gather_kernel, depth, half),
+        functools.partial(gather_attend_kernel, depth, half, scale),
         out_shape=(
-            jax.ShapeDtypeStruct((blocks,) + keys.shape, keys.dtype),
-            jax.ShapeDtypeStruct((blocks,) + values.shape, values.dtype),
+            jax.ShapeDtypeStruct(queries.shape, queries.dtype),
             jax.ShapeDtypeStruct((depth, half, weight.shape[1]), weight.dtype),
         ),
-        in_specs=[anywhere] * 3,
-        out_specs=(anywhere,) * 3,
+        in_specs=[pl.BlockSpec(memory_space=pltpu.SMEM), vmem, vmem, vmem, anywhere],
+        out_specs=(vmem, anywhere),
         scratch_shapes=[
-            dma((3,)), dma((2, depth, 2)), dma((2, depth, 2)), dma((2, depth)),
+            pltpu.VMEM((blocks,) + keys.shape, keys.dtype),
+            pltpu.VMEM((blocks,) + values.shape, values.dtype),
+            pltpu.VMEM((heads, HEAD_FEATURES, rows), queries.dtype),
+            pltpu.VMEM((heads, 1, rows), jnp.float32),
+            pltpu.VMEM((heads, 1, rows), jnp.float32),
+            pltpu.VMEM((heads, HEAD_FEATURES, rows), jnp.float32),
+            dma((1,)), dma((2, depth, 2)), dma((2, depth, 2)), dma((2, depth)),
             dma((2, blocks)), dma((depth, 2)), dma((depth,)),
         ],
         compiler_params=pltpu.CompilerParams(
             collective_id=0, has_side_effects=True, vmem_limit_bytes=vmem_limit
         ),
-    )(keys, values, weight)
+    )(placement, queries, keys, values, weight)
 
 
 def project_kernel(depth, half, hid_ref, w_ref, w_first, out_ref,
@@ -443,13 +530,11 @@
     table = jnp.arange(blocks, dtype=jnp.int32)
     own_block = jnp.sum(jnp.where(table == lax.axis_index("ctx"), placement, 0))[None]
     if fast:
-        all_keys, all_values, w_first = gather(depth, half, keys, values, weight)
-    else:
-        all_keys = lax.all_gather(keys, "ctx", axis=0)
-        all_values = lax.all_gather(values, "ctx", axis=0)
+        hidden, w_first = gather_attend(depth, half, placement, queries, keys, values, weight)
+        return project(depth, half, hidden, weight, w_first)
+    all_keys = lax.all_gather(keys, "ctx", axis=0)
+    all_values = lax.all_gather(values, "ctx", axis=0)
     hidden = attend(placement, own_block, queries, all_keys, all_values)
-    if fast:
-        return project(depth, half, hidden, weight, w_first)
     partial_sum = jnp.dot(
         hidden,
         lax.all_gather(weight, "ctx", axis=1, tiled=True),

time: 226 us -> 156 us (0.69)
  Pallas kernels: 223 us -> 153 us
    pallas_call x1, Pallas kernels: 135 us -> 60.5 us  [project(): pl.pallas_call(functools.partial(project_kernel, depth, half), out_shape=...]
    pallas_call x2 -> x1, Pallas kernels: 88 us -> 92.6 us  [gather_attend(): pl.pallas_call(functools.partial(gather_attend_kernel, depth, half, scale...]
where the time goes in v2:
time: 156 us; the launch traced here: 155 us
  Pallas kernels  153 us (98%)
  local copies, waits for them, and re-layouts  2.3 us (1%)
    pallas_call x1, Pallas kernels, gather_attend(): pl.pallas_call(functools.partial(gather_attend_kernel, depth, half, scale...  92.6 us
    pallas_call x1, Pallas kernels, project(): pl.pallas_call(functools.partial(project_kernel, depth, half), out_shape=...  60.5 us

profile of v2, /device:TPU:0, one launch (start us, length us, event | category | flops | bytes accessed | tf_op | source)
XLA Modules:
  0.0 155.4 jit_solution(2515677314014126581)
XLA Ops:
  0.0 92.6 %shard_map.55 = (bf16[256,2048]{1,0:T(8,128)(2,1)}, bf16[4,1024,256]{2,1,0:T(8,128)(2,1)}) custom-call(s32[16]{0:T(128)} %place_ref.1, bf16[256,2048]{1,0:T(8,128)(2,1)} %q_ref.1, bf16[256,512]{1,0:T(8,128)(2,1)} %k_ref.1, bf16[256,512]{1,0:T(8,128)(2,1)} %v_ref.1, bf16[2048,256]{1,0:T(8,128)(2,1)} %w_ref.3), custom_call_target="tpu_custom_call" | custom-call | tf_op jit(solution)/shard_map/pallas_call | solution.py:346
  92.6 60.5 %shard_map.56 = bf16[256,2048]{1,0:T(8,128)(2,1)} custom-call(bf16[256,2048]{1,0:T(8,128)(2,1)} %get-tuple-element.7.hid_ref, bf16[2048,256]{1,0:T(8,128)(2,1)} %w_ref.3, bf16[4,1024,256]{2,1,0:T(8,128)(2,1)} %get-tuple-element.8.w_first), custom_call_target="tpu_custom_call" | custom-call | tf_op jit(solution)/shard_map/pallas_call | solution.py:508
  153.1 2.3 %copy.7 = bf16[256,2048]{1,0:T(8,128)(2,1)} copy(bf16[256,2048]{1,0:T(8,128)(2,1)} %shard_map.56) | data formatting | bytes 2097152

commit v3 on v2

--- a/solution.py
+++ b/solution.py
@@ -136,7 +136,7 @@
     )
 
 
-def gather_attend_kernel(depth, half, scale, place_ref, q_ref, k_ref, v_ref, w_ref, o_ref, w_all,
+def gather_attend_kernel(depth, early, scale, place_ref, q_ref, k_ref, v_ref, w_ref, o_ref, w_all,
                          k_all, v_all, turned, peak, total, acc,
                          own_sem, line_send, plane_send, relay_send, recv, w_send, w_recv):
     z, p, px, py, pd = place_of(depth)
@@ -150,7 +150,7 @@
         pl.semaphore_signal(barrier, inc=1, device_id={"ctx": other}, device_id_type=MESH)
     pl.semaphore_wait(barrier, len(greeted))
 
-    w_own = w_ref.at[pl.ds(0, half), :]
+    w_own = w_ref.at[pl.ds(0, early), :]
     w_local = pltpu.make_async_copy(w_own, w_all.at[z], own_sem.at[0])
     copies = Copies()
     pairs = ((k_ref, k_all), (v_ref, v_all))
@@ -245,41 +245,39 @@
         return slice(h * HEAD_FEATURES, (h + 1) * HEAD_FEATURES)
 
     for h in range(heads):
-        turned[h] = q_ref[:, features(h)].T
+        at = h % common * rows
+        turned[h // common, :, at:at + rows] = q_ref[:, features(h)].T
 
     def update(read_keys, read_values, bias, first):
-        def score(h):
-            return jnp.dot(
-                read_keys(features(h // common)), turned[h], preferred_element_type=jnp.float32
-            )
+        def score(g):
+            return jnp.dot(read_keys(features(g)), turned[g], preferred_element_type=jnp.float32)
 
         following = score(0)
-        for h in range(heads):
+        for g in range(heads // common):
             scores = following
-            if h + 1 < heads:
-                following = score(h + 1)
-            if h % common == 0:
-                values = read_values(features(h // common)).T
+            if g + 1 < heads // common:
+                following = score(g + 1)
+            values = read_values(features(g)).T
             if first:
                 key_at = lax.broadcasted_iota(jnp.int32, scores.shape, 0)
-                query_at = lax.broadcasted_iota(jnp.int32, scores.shape, 1)
+                query_at = lax.broadcasted_iota(jnp.int32, scores.shape, 1) % rows
                 scores = jnp.where(key_at <= query_at, scores, lowest)
                 new = jnp.max(scores, axis=0, keepdims=True)
                 weights = jnp.exp2((scores - new) * scale)
             else:
-                old = peak[h]
+                old = peak[g]
                 new = jnp.maximum(old, jnp.max(scores, axis=0, keepdims=True) + bias)
                 weights = jnp.exp2((scores - (new - bias)) * scale)
                 shrink = jnp.exp2((old - new) * scale)
             sums = jnp.sum(weights, axis=0, keepdims=True)
             part = jnp.dot(values, weights.astype(jnp.bfloat16), preferred_element_type=jnp.float32)
-            peak[h] = new
+            peak[g] = new
             if first:
-                total[h] = sums
-                acc[h] = part
+                total[g] = sums
+                acc[g] = part
             else:
-                total[h] = total[h] * shrink + sums
-                acc[h] = acc[h] * shrink + part
+                total[g] = total[g] * shrink + sums
+                acc[g] = acc[g] * shrink + part
 
     update(lambda f: k_ref[:, f], lambda f: v_ref[:, f], 0.0, True)
     pass_on(1)
@@ -330,34 +328,37 @@
 
     lax.fori_loop(1, depth * PLANE, step, 0)
     for h in range(heads):
-        o_ref[:, features(h)] = (acc[h] / total[h]).T.astype(o_ref.dtype)
+        cols = slice(h % common * rows, (h % common + 1) * rows)
+        out = acc[h // common, :, cols] / total[h // common, :, cols]
+        o_ref[:, features(h)] = out.T.astype(o_ref.dtype)
     w_local.wait()
     copies.finish()
 
 
-def gather_attend(depth, half, placement, queries, keys, values, weight):
+def gather_attend(depth, early, placement, queries, keys, values, weight):
     blocks = depth * PLANE
     rows = queries.shape[0]
-    heads = queries.shape[1] // HEAD_FEATURES
+    groups = keys.shape[1] // HEAD_FEATURES
+    lanes = rows * queries.shape[1] // keys.shape[1]
     scale = HEAD_FEATURES ** (-0.5) * LOG2_E
     dma = pltpu.SemaphoreType.DMA
     anywhere = pl.BlockSpec(memory_space=pl.ANY)
     vmem = pl.BlockSpec(memory_space=pltpu.VMEM)
     return pl.pallas_call(
-        functools.partial(gather_attend_kernel, depth, half, scale),
+        functools.partial(gather_attend_kernel, depth, early, scale),
         out_shape=(
             jax.ShapeDtypeStruct(queries.shape, queries.dtype),
-            jax.ShapeDtypeStruct((depth, half, weight.shape[1]), weight.dtype),
+            jax.ShapeDtypeStruct((depth, early, weight.shape[1]), weight.dtype),
         ),
         in_specs=[pl.BlockSpec(memory_space=pltpu.SMEM), vmem, vmem, vmem, anywhere],
         out_specs=(vmem, anywhere),
         scratch_shapes=[
             pltpu.VMEM((blocks,) + keys.shape, keys.dtype),
             pltpu.VMEM((blocks,) + values.shape, values.dtype),
-            pltpu.VMEM((heads, HEAD_FEATURES, rows), queries.dtype),
-            pltpu.VMEM((heads, 1, rows), jnp.float32),
-            pltpu.VMEM((heads, 1, rows), jnp.float32),
-            pltpu.VMEM((heads, HEAD_FEATURES, rows), jnp.float32),
+            pltpu.VMEM((groups, HEAD_FEATURES, lanes), queries.dtype),
+            pltpu.VMEM((groups, 1, lanes), jnp.float32),
+            pltpu.VMEM((groups, 1, lanes), jnp.float32),
+            pltpu.VMEM((groups, HEAD_FEATURES, lanes), jnp.float32),
             dma((1,)), dma((2, depth, 2)), dma((2, depth, 2)), dma((2, depth)),
             dma((2, blocks)), dma((depth, 2)), dma((depth,)),
         ],
@@ -392,7 +393,8 @@
     above = z + 1 < depth
     below = z > 0
     own_parts = [hid_ref.at[:, pl.ds(s * half, half)] for s in range(2)]
-    w_own = w_ref.at[pl.ds(half, half), :]
+    early = w_first.shape[1]
+    w_own = w_ref.at[pl.ds(early, 2 * half - early), :]
 
     def send_hidden(part, axis):
         target = z * PLANE + (px if axis == 0 else py)
@@ -436,7 +438,7 @@
 
     for t in range(1, depth):
         pass_weight(t)
-        if t == 1:
+        if t == 2:
             for part in range(2):
                 hidden_arrived(px if part == 0 else py, part)
                 copies.start(always, functools.partial(relay_hidden, part))
@@ -445,8 +447,15 @@
 
     def term(source, chunk):
         return (
-            jnp.dot(hid[source, 0], w_first[chunk], preferred_element_type=jnp.float32)
-            + jnp.dot(hid[source, 1], w_late[chunk], preferred_element_type=jnp.float32)
+            jnp.dot(hid[source, 0], w_first[chunk, :half], preferred_element_type=jnp.float32)
+            + jnp.dot(
+                hid[source, 1, :, :early - half], w_first[chunk, half:],
+                preferred_element_type=jnp.float32,
+            )
+            + jnp.dot(
+                hid[source, 1, :, early - half:], w_late[chunk],
+                preferred_element_type=jnp.float32,
+            )
         ).astype(jnp.bfloat16)
 
     def core_copy(slot):
@@ -512,7 +521,7 @@
         out_specs=vmem,
         scratch_shapes=[
             pltpu.VMEM((PLANE, 2, rows, half), jnp.bfloat16),
-            pltpu.VMEM((depth, half, cols), jnp.bfloat16),
+            pltpu.VMEM((depth, 2 * half - w_first.shape[1], cols), jnp.bfloat16),
             block, block, block, block, block,
             dma((3,)), dma((2, 2)), dma((2,)), dma((PLANE, 2)), dma((depth, 2)), dma((depth,)),
             dma((PLANE,)), dma((PLANE,)), dma((PLANE,)), dma((PLANE,)),
@@ -527,10 +536,11 @@
     blocks = placement.shape[0]
     depth = blocks // PLANE
     half = weight.shape[0] // 2
+    early = half + half // 2
     table = jnp.arange(blocks, dtype=jnp.int32)
     own_block = jnp.sum(jnp.where(table == lax.axis_index("ctx"), placement, 0))[None]
     if fast:
-        hidden, w_first = gather_attend(depth, half, placement, queries, keys, values, weight)
+        hidden, w_first = gather_attend(depth, early, placement, queries, keys, values, weight)
         return project(depth, half, hidden, weight, w_first)
     all_keys = lax.all_gather(keys, "ctx", axis=0)
     all_values = lax.all_gather(values, "ctx", axis=0)

time: 156 us -> 161 us (1.032)
  Pallas kernels: 153 us -> 159 us
    pallas_call x1, Pallas kernels: 92.6 us -> 104 us  [gather_attend(): pl.pallas_call(functools.partial(gather_attend_kernel, depth, early, scal...]
    pallas_call x1, Pallas kernels: 60.5 us -> 55.1 us  [project(): pl.pallas_call(functools.partial(project_kernel, depth, half), out_shape=...]
where the time goes in v3:
time: 161 us
  Pallas kernels  159 us (99%)
  local copies, waits for them, and re-layouts  2.3 us (1%)
    pallas_call x1, Pallas kernels, gather_attend(): pl.pallas_call(functools.partial(gather_attend_kernel, depth, early, scal...  104 us
    pallas_call x1, Pallas kernels, project(): pl.pallas_call(functools.partial(project_kernel, depth, half), out_shape=...  55.1 us

profile of v3, /device:TPU:0, one launch (start us, length us, event | category | flops | bytes accessed | tf_op | source)
XLA Modules:
  0.0 161.0 jit_solution(13760590870295112970)
XLA Ops:
  0.0 103.5 %shard_map.55 = (bf16[256,2048]{1,0:T(8,128)(2,1)}, bf16[4,1536,256]{2,1,0:T(8,128)(2,1)}) custom-call(s32[16]{0:T(128)} %place_ref.1, bf16[256,2048]{1,0:T(8,128)(2,1)} %q_ref.1, bf16[256,512]{1,0:T(8,128)(2,1)} %k_ref.1, bf16[256,512]{1,0:T(8,128)(2,1)} %v_ref.1, bf16[2048,256]{1,0:T(8,128)(2,1)} %w_ref.3), custom_call_target="tpu_custom_call" | custom-call | tf_op jit(solution)/shard_map/pallas_call | solution.py:347
  103.5 55.1 %shard_map.56 = bf16[256,2048]{1,0:T(8,128)(2,1)} custom-call(bf16[256,2048]{1,0:T(8,128)(2,1)} %get-tuple-element.7.hid_ref, bf16[2048,256]{1,0:T(8,128)(2,1)} %w_ref.3, bf16[4,1536,256]{2,1,0:T(8,128)(2,1)} %get-tuple-element.8.w_first), custom_call_target="tpu_custom_call" | custom-call | tf_op jit(solution)/shard_map/pallas_call | solution.py:517
  158.7 2.3 %copy.7 = bf16[256,2048]{1,0:T(8,128)(2,1)} copy(bf16[256,2048]{1,0:T(8,128)(2,1)} %shard_map.56) | data formatting | bytes 2097152

commit v4 on v3

--- a/solution.py
+++ b/solution.py
@@ -137,7 +137,7 @@
 
 
 def gather_attend_kernel(depth, early, scale, place_ref, q_ref, k_ref, v_ref, w_ref, o_ref, w_all,
-                         k_all, v_all, turned, peak, total, acc,
+                         k_all, v_all, turned, peak, acc,
                          own_sem, line_send, plane_send, relay_send, recv, w_send, w_recv):
     z, p, px, py, pd = place_of(depth)
     me = z * PLANE + p
@@ -248,6 +248,8 @@
         at = h % common * rows
         turned[h // common, :, at:at + rows] = q_ref[:, features(h)].T
 
+    ones = jnp.ones((16, rows), v_ref.dtype)
+
     def update(read_keys, read_values, bias, first):
         def score(g):
             return jnp.dot(read_keys(features(g)), turned[g], preferred_element_type=jnp.float32)
@@ -257,7 +259,7 @@
             scores = following
             if g + 1 < heads // common:
                 following = score(g + 1)
-            values = read_values(features(g)).T
+            values = jnp.concatenate([read_values(features(g)).T, ones], axis=0)
             if first:
                 key_at = lax.broadcasted_iota(jnp.int32, scores.shape, 0)
                 query_at = lax.broadcasted_iota(jnp.int32, scores.shape, 1) % rows
@@ -269,14 +271,11 @@
                 new = jnp.maximum(old, jnp.max(scores, axis=0, keepdims=True) + bias)
                 weights = jnp.exp2((scores - (new - bias)) * scale)
                 shrink = jnp.exp2((old - new) * scale)
-            sums = jnp.sum(weights, axis=0, keepdims=True)
             part = jnp.dot(values, weights.astype(jnp.bfloat16), preferred_element_type=jnp.float32)
             peak[g] = new
             if first:
-                total[g] = sums
                 acc[g] = part
             else:
-                total[g] = total[g] * shrink + sums
                 acc[g] = acc[g] * shrink + part
 
     update(lambda f: k_ref[:, f], lambda f: v_ref[:, f], 0.0, True)
@@ -329,7 +328,8 @@
     lax.fori_loop(1, depth * PLANE, step, 0)
     for h in range(heads):
         cols = slice(h % common * rows, (h % common + 1) * rows)
-        out = acc[h // common, :, cols] / total[h // common, :, cols]
+        total = acc[h // common, HEAD_FEATURES:HEAD_FEATURES + 1, cols]
+        out = acc[h // common, :HEAD_FEATURES, cols] / total
         o_ref[:, features(h)] = out.T.astype(o_ref.dtype)
     w_local.wait()
     copies.finish()
@@ -357,8 +357,7 @@
             pltpu.VMEM((blocks,) + values.shape, values.dtype),
             pltpu.VMEM((groups, HEAD_FEATURES, lanes), queries.dtype),
             pltpu.VMEM((groups, 1, lanes), jnp.float32),
-            pltpu.VMEM((groups, 1, lanes), jnp.float32),
-            pltpu.VMEM((groups, HEAD_FEATURES, lanes), jnp.float32),
+            pltpu.VMEM((groups, HEAD_FEATURES + 16, lanes), jnp.float32),
             dma((1,)), dma((2, depth, 2)), dma((2, depth, 2)), dma((2, depth)),
             dma((2, blocks)), dma((depth, 2)), dma((depth,)),
         ],
@@ -438,7 +437,7 @@
 
     for t in range(1, depth):
         pass_weight(t)
-        if t == 2:
+        if t == 1:
             for part in range(2):
                 hidden_arrived(px if part == 0 else py, part)
                 copies.start(always, functools.partial(relay_hidden, part))
@@ -536,7 +535,7 @@
     blocks = placement.shape[0]
     depth = blocks // PLANE
     half = weight.shape[0] // 2
-    early = half + half // 2
+    early = half + half // 4
     table = jnp.arange(blocks, dtype=jnp.int32)
     own_block = jnp.sum(jnp.where(table == lax.axis_index("ctx"), placement, 0))[None]
     if fast:

time: 161 us -> 152 us (0.944)
  Pallas kernels: 159 us -> 149 us
    pallas_call x1, Pallas kernels: 104 us -> 94.2 us  [gather_attend(): pl.pallas_call(functools.partial(gather_attend_kernel, depth, early, scal...]
where the time goes in v4:
time: 152 us
  Pallas kernels  149 us (98%)
  local copies, waits for them, and re-layouts  2.3 us (2%)
    pallas_call x1, Pallas kernels, gather_attend(): pl.pallas_call(functools.partial(gather_attend_kernel, depth, early, scal...  94.2 us
    pallas_call x1, Pallas kernels, project(): pl.pallas_call(functools.partial(project_kernel, depth, half), out_shape=...  55 us

profile of v4, /device:TPU:0, one launch (start us, length us, event | category | flops | bytes accessed | tf_op | source)
XLA Modules:
  0.0 151.6 jit_solution(6555824183699848287)
XLA Ops:
  0.0 94.2 %shard_map.55 = (bf16[256,2048]{1,0:T(8,128)(2,1)}, bf16[4,1280,256]{2,1,0:T(8,128)(2,1)}) custom-call(s32[16]{0:T(128)} %place_ref.1, bf16[256,2048]{1,0:T(8,128)(2,1)} %q_ref.1, bf16[256,512]{1,0:T(8,128)(2,1)} %k_ref.1, bf16[256,512]{1,0:T(8,128)(2,1)} %v_ref.1, bf16[2048,256]{1,0:T(8,128)(2,1)} %w_ref.3), custom_call_target="tpu_custom_call" | custom-call | tf_op jit(solution)/shard_map/pallas_call | solution.py:347
  94.3 55.0 %shard_map.56 = bf16[256,2048]{1,0:T(8,128)(2,1)} custom-call(bf16[256,2048]{1,0:T(8,128)(2,1)} %get-tuple-element.7.hid_ref, bf16[2048,256]{1,0:T(8,128)(2,1)} %w_ref.3, bf16[4,1280,256]{2,1,0:T(8,128)(2,1)} %get-tuple-element.8.w_first), custom_call_target="tpu_custom_call" | custom-call | tf_op jit(solution)/shard_map/pallas_call | solution.py:516
  149.3 2.3 %copy.7 = bf16[256,2048]{1,0:T(8,128)(2,1)} copy(bf16[256,2048]{1,0:T(8,128)(2,1)} %shard_map.56) | data formatting | bytes 2097152

commit v5 on v4

--- a/solution.py
+++ b/solution.py
@@ -290,8 +290,9 @@
         3: ((pass_on, 2),),
         4: ((pass_across, 1), (pass_weight, 1)),
         6: ((pass_on, 3),),
-        8: ((pass_across, 2), (pass_weight, 2)),
-        12: ((pass_across, 3), (pass_weight, 3)),
+        8: ((pass_across, 2),),
+        9: ((pass_weight, 2),),
+        12: ((pass_across, 3),),
     }
 
     def step(n, carry):
@@ -331,6 +332,7 @@
         total = acc[h // common, HEAD_FEATURES:HEAD_FEATURES + 1, cols]
         out = acc[h // common, :HEAD_FEATURES, cols] / total
         o_ref[:, features(h)] = out.T.astype(o_ref.dtype)
+    pass_weight(3)
     w_local.wait()
     copies.finish()
 

time: 152 us -> 146 us (0.961)
  Pallas kernels: 149 us -> 143 us
    pallas_call x1, Pallas kernels: 94.2 us -> 87.3 us  [gather_attend(): pl.pallas_call(functools.partial(gather_attend_kernel, depth, early, scal...]
where the time goes in v5:
time: 146 us; the launch traced here: 145 us
  Pallas kernels  143 us (98%)
  local copies, waits for them, and re-layouts  2.3 us (2%)
    pallas_call x1, Pallas kernels, gather_attend(): pl.pallas_call(functools.partial(gather_attend_kernel, depth, early, scal...  87.3 us
    pallas_call x1, Pallas kernels, project(): pl.pallas_call(functools.partial(project_kernel, depth, half), out_shape=...  55.8 us

profile of v5, /device:TPU:0, one launch (start us, length us, event | category | flops | bytes accessed | tf_op | source)
XLA Modules:
  0.0 145.4 jit_solution(9747598916559180265)
XLA Ops:
  0.0 87.3 %shard_map.55 = (bf16[256,2048]{1,0:T(8,128)(2,1)}, bf16[4,1280,256]{2,1,0:T(8,128)(2,1)}) custom-call(s32[16]{0:T(128)} %place_ref.1, bf16[256,2048]{1,0:T(8,128)(2,1)} %q_ref.1, bf16[256,512]{1,0:T(8,128)(2,1)} %k_ref.1, bf16[256,512]{1,0:T(8,128)(2,1)} %v_ref.1, bf16[2048,256]{1,0:T(8,128)(2,1)} %w_ref.3), custom_call_target="tpu_custom_call" | custom-call | tf_op jit(solution)/shard_map/pallas_call | solution.py:349
  87.3 55.8 %shard_map.56 = bf16[256,2048]{1,0:T(8,128)(2,1)} custom-call(bf16[256,2048]{1,0:T(8,128)(2,1)} %get-tuple-element.7.hid_ref, bf16[2048,256]{1,0:T(8,128)(2,1)} %w_ref.3, bf16[4,1280,256]{2,1,0:T(8,128)(2,1)} %get-tuple-element.8.w_first), custom_call_target="tpu_custom_call" | custom-call | tf_op jit(solution)/shard_map/pallas_call | solution.py:518
  143.1 2.3 %copy.7 = bf16[256,2048]{1,0:T(8,128)(2,1)} copy(bf16[256,2048]{1,0:T(8,128)(2,1)} %shard_map.56) | data formatting | bytes 2097152
